TPU v7x, 32 devices: a whole 2x2x4 slice. The times are simulated.
32 devices in a mesh: rep: 8 (over z, y), shard: 4 (over x, core).
Axes of the slice: x: 2, y: 2, z: 4, core: 2. Of those that a mesh axis runs over, the one named last changes fastest.
Arguments:
- gradient: bfloat16 [8, 1024, 4096], P('rep', None, 'shard'), may hold values from -16 to 16
- feedback: bfloat16 [8, 1024, 4096], P('rep', None, 'shard'), may hold values from -4 to 4
- warm_start: float32 [1024, 64], replicated, may hold values from -6 to 6
- master: float32 [1024, 4096], P('rep', 'shard'), may hold values from -4 to 4
- moment: float32 [1024, 4096], P('rep', 'shard'), may hold values from -1.5 to 1.5
- second: float32 [1024, 4096], P('rep', 'shard'), may hold values from 0.005 to 0.5
Outputs:
- new_feedback: bfloat16 [8, 1024, 4096], P('rep', None, 'shard')
- weights: bfloat16 [1024, 4096], P(None, 'shard')
- master_out: float32 [1024, 4096], P('rep', 'shard')
- moment_out: float32 [1024, 4096], P('rep', 'shard')
- second_out: float32 [1024, 4096], P('rep', 'shard')
- right_factor: float32 [1024, 64], replicated
All inputs are finite; a program needn't handle non-finite values.
Results may differ from a plain program's by a relative error of at most 0.001.
Values may be sent and summed in bfloat16 or wider, within the bound.
A program may use at most 64 MiB of HBM per device.

v0:
```python
import jax
import jax.numpy as jnp
from jax import lax
from jax.sharding import PartitionSpec as P

HIGHEST = lax.Precision.HIGHEST
beta_one = 0.9
beta_two = 0.95
learn_rate = 0.02
decay_rate = 0.1
adam_eps = 1e-08
ridge_rate = 1e-06


def lower_inverse(gram):
    matrix_order = gram.shape[0]
    identity = jnp.eye(matrix_order, dtype=jnp.float32)
    ridge_term = ridge_rate * jnp.trace(gram) / matrix_order
    cholesky_lower = jnp.linalg.cholesky(gram + ridge_term * identity)
    return jax.scipy.linalg.solve_triangular(cholesky_lower, identity, lower=True)


def contract_first(left, right):
    return lax.dot_general(
        left, right, (((0,), (0,)), ((), ())), precision=HIGHEST, preferred_element_type=jnp.float32
    )


def times_inverse(left, inverse):
    return jnp.dot(left, inverse.T, precision=HIGHEST, preferred_element_type=jnp.float32)


def on_device(gradient, feedback, warm_start, master, moment, second):
    replicas = lax.axis_size("rep")
    merged = gradient[0].astype(jnp.float32) + feedback[0].astype(jnp.float32)
    local_factor = contract_first(merged, warm_start)
    factor = lax.psum(local_factor, "rep") / replicas
    gram_part = contract_first(factor, factor)
    gram = lax.psum(gram_part, "shard")
    inverse = lower_inverse(gram)
    unit_basis = times_inverse(factor, inverse)
    projected = jnp.dot(merged, unit_basis, precision=HIGHEST, preferred_element_type=jnp.float32)
    right_factor = lax.psum(projected, ("rep", "shard")) / replicas
    approx = lax.dot_general(
        right_factor,
        unit_basis,
        (((1,), (1,)), ((), ())),
        precision=HIGHEST,
        preferred_element_type=jnp.float32,
    )
    new_feedback = (merged - approx).astype(jnp.bfloat16)[None]
    own_rows = master.shape[0]
    row_start = lax.axis_index("rep") * own_rows
    grad_rows = lax.dynamic_slice_in_dim(approx, row_start, own_rows, 0)
    moment_out = beta_one * moment + (1.0 - beta_one) * grad_rows
    second_out = beta_two * second + (1.0 - beta_two) * grad_rows * grad_rows
    master_out = master - learn_rate * (
        moment_out / (jnp.sqrt(second_out) + adam_eps) + decay_rate * master
    )
    weights = lax.all_gather(master_out.astype(jnp.bfloat16), "rep", axis=0, tiled=True)
    return (new_feedback, weights, master_out, moment_out, second_out, right_factor)


def solution(mesh):
    return jax.shard_map(
        on_device,
        mesh=mesh,
        in_specs=(
            P("rep", None, "shard"),
            P("rep", None, "shard"),
            P(),
            P("rep", "shard"),
            P("rep", "shard"),
            P("rep", "shard"),
        ),
        out_specs=(
            P("rep", None, "shard"),
            P(None, "shard"),
            P("rep", "shard"),
            P("rep", "shard"),
            P("rep", "shard"),
            P(),
        ),
        check_vma=False,
    )
```

profile of v0, /device:TPU:0, one launch (start us, length us, event | category | flops | bytes accessed | tf_op | source)
XLA Modules:
  0.0 312.0 jit_solution(17606568645292619925)
XLA Ops:
  7.2 0.0 copy-start
  7.2 0.0 copy-start.2
  7.2 0.0 all-reduce.3.cloned.1.call-start
  7.2 0.9 copy-done
  8.1 6.1 %fusion.2 = f32[1024,64]{0,1:T(8,128)} fusion(f32[1024,64]{0,1:T(8,128)S(1)} %copy-done, bf16[1,1024,1024]{2,1,0:T(8,128)(2,1)} %param.7, bf16[1,1024,1024]{2,1,0:T(8,128)(2,1)} %param.6), kind=kOutput, calls=%fused_computation.3 | convolution fusion | flops 808452096 | bytes 4718592 | tf_op jit(solution)/shard_map/dot_general | solution.py:24
  14.2 0.0 all-reduce.3.cloned.1.call-update
  14.2 0.0 all-reduce.5.cloned.1.call-start
  14.3 73.4 %all-reduce.3.cloned.1.call-done = f32[1024,64]{0,1:T(8,128)} async-done(((f32[1024,64]{0,1:T(8,128)}), f32[1024,64]{0,1:T(8,128)}) %all-reduce.3.cloned.1.call-update) | async-done | bytes 262160 | tf_op jit(solution)/shard_map/psum | solution.py:37
  87.6 1.4 fusion.9
  89.0 10.3 %psum.22 = f32[64,64]{1,0:T(8,128)S(1)} all-reduce(f32[64,64]{1,0:T(8,128)S(1)} %fusion.9), channel_id=1, replica_groups=mesh['rep'=8,'shard'=4] {'shard'}, use_global_device_ids=true, to_apply=%region_1.0 | all-reduce | flops 4096 | bytes 32768 | tf_op jit(solution)/shard_map/psum | solution.py:39
  99.3 0.6 select_reduce_fusion.1
  100.6 0.1 copy.12
  100.7 5.8 %cholesky.18 = f32[64,64]{1,0:T(8,128)S(1)} custom-call(f32[64,64]{1,0:T(8,128)S(1)} %fusion.16), custom_call_target="Cholesky" | custom-call | tf_op jit(solution)/shard_map/jit(cholesky)/cholesky | solution.py:19
  106.6 0.6 compare_reduce_fusion
  107.2 0.7 fusion.13
  107.9 4.9 %custom-call.7 = f32[1,64,64]{1,2,0:T(8,128)S(1)} custom-call(f32[1,64,64]{2,1,0:T(8,128)S(1)} %fusion.13), custom_call_target="InvertDiagBlocksLowerTriangular" | custom-call | tf_op jit(solution)/shard_map/jit(_solve_triangular)/triangular_solve | solution.py:20
  112.8 0.2 fusion.14
  113.0 1.3 fusion.7
  114.3 0.0 copy-done.2
  114.3 0.0 copy-start.4
  114.4 6.9 %fusion = f32[1024,64]{0,1:T(8,128)} fusion(f32[1024,64]{0,1:T(8,128)S(1)} %fusion.7, bf16[1,1024,1024]{2,1,0:T(8,128)(2,1)S(1)} %copy-done.2, bf16[1,1024,1024]{2,1,0:T(8,128)(2,1)} %param.6), kind=kOutput, calls=%fused_computation.1 | convolution fusion | flops 808452096 | bytes 4718592 | tf_op jit(solution)/shard_map/dot_general | solution.py:42
  121.2 0.0 all-reduce.5.cloned.1.call-update
  121.3 0.2 all-gather.2.cloned.1.call-start
  121.5 124.4 %all-reduce.5.cloned.1.call-done = f32[1024,64]{0,1:T(8,128)} async-done(((f32[1024,64]{0,1:T(8,128)}), f32[1024,64]{0,1:T(8,128)}) %all-reduce.5.cloned.1.call-update) | async-done | bytes 262160 | tf_op jit(solution)/shard_map/psum | solution.py:43
  245.9 0.0 copy-start.5
  245.9 0.0 copy-start.6
  245.9 1.1 broadcast_multiply_fusion
  247.0 0.0 copy-start.3
  247.0 3.5 %fusion.21 = f32[1024,1024]{1,0:T(8,128)S(1)} fusion(f32[1024,64]{0,1:T(8,128)S(1)} %broadcast_multiply_fusion, f32[1024,64]{0,1:T(8,128)S(1)} %fusion.7), kind=kOutput, calls=%fused_computation.34 | convolution fusion | flops 805306368 | bytes 4718592 | tf_op jit(solution)/shard_map/dot_general | solution.py:44
  250.5 0.0 copy-start.1
  250.5 1.9 copy-done.1
  252.4 0.0 copy-done.4
  252.4 0.0 copy-done.5
  252.4 0.0 copy-done.6
  252.4 1.5 fusion.19
  253.9 0.0 copy-done.3
  253.9 0.0 all-gather.2.cloned.1.call-update
  254.0 5.4 %fusion.5 = bf16[1,1024,1024]{2,1,0:T(8,128)(2,1)} fusion(f32[1024,1024]{1,0:T(8,128)} %copy-done.1, bf16[1,1024,1024]{2,1,0:T(8,128)(2,1)S(1)} %copy-done.2, bf16[1,1024,1024]{2,1,0:T(8,128)(2,1)} %param.6), kind=kLoop, calls=%fused_computation.7 | loop fusion | flops 5242880 | bytes 10485760 | tf_op jit(solution)/shard_map/broadcast_in_dim | solution.py:51
  259.4 43.1 %all-gather.2.cloned.1.call-done = bf16[1024,1024]{1,0:T(8,128)(2,1)} async-done(((bf16[128,1024]{1,0:T(8,128)(2,1)}), bf16[1024,1024]{1,0:T(8,128)(2,1)}) %all-gather.2.cloned.1.call-update) | async-done | bytes 2097168 | tf_op jit(solution)/shard_map/all_gather | solution.py:60
  302.4 3.1 copy.16
  (3 shorter events, 0.1 us)
Async XLA Ops:
  7.2 1.0 copy-start
  7.2 107.2 %copy-start.2 = (bf16[1,1024,1024]{2,1,0:T(8,128)(2,1)S(1)}, bf16[1,1024,1024]{2,1,0:T(8,128)(2,1)}, u32[]{:S(2)}) copy-start(bf16[1,1024,1024]{2,1,0:T(8,128)(2,1)} %param.7) | copy-start | bytes 6291460
  7.2 80.4 %all-reduce.3.cloned.1.call-start = ((), (), s32[]{:S(2)}) async-start(), calls=%async_computation | async-start | bytes 524288 | tf_op jit(solution)/shard_map/psum | solution.py:37
  14.2 231.7 %all-reduce.5.cloned.1.call-start = ((), (), s32[]{:S(2)}) async-start(), calls=%async_computation.1 | async-start | bytes 524288 | tf_op jit(solution)/shard_map/psum | solution.py:43
  114.3 138.1 %copy-start.4 = (f32[128,1024]{1,0:T(8,128)S(1)}, f32[128,1024]{1,0:T(8,128)}, u32[]{:S(2)}) copy-start(f32[128,1024]{1,0:T(8,128)} %param.9) | copy-start | bytes 1572868
  121.3 181.2 %all-gather.2.cloned.1.call-start = ((), (), s32[]{:S(2)}) async-start(), calls=%async_computation.2 | async-start | bytes 2359296 | tf_op jit(solution)/shard_map/all_gather | solution.py:60
  245.9 6.5 %copy-start.5 = (f32[128,1024]{1,0:T(8,128)S(1)}, f32[128,1024]{1,0:T(8,128)}, u32[]{:S(2)}) copy-start(f32[128,1024]{1,0:T(8,128)} %param.11) | copy-start | bytes 1572868
  245.9 6.5 %copy-start.6 = (f32[128,1024]{1,0:T(8,128)S(1)}, f32[128,1024]{1,0:T(8,128)}, u32[]{:S(2)}) copy-start(f32[128,1024]{1,0:T(8,128)} %param.10) | copy-start | bytes 1572868
  247.0 7.0 %copy-start.3 = (f32[1024,64]{0,1:T(8,128)}, f32[1024,64]{0,1:T(8,128)S(1)}, u32[]{:S(2)}) copy-start(f32[1024,64]{0,1:T(8,128)S(1)} %broadcast_multiply_fusion) | copy-start | bytes 786436
  250.5 1.9 copy-start.1
Sparse Core Ops, SparseCore 0:
  14.3 73.2 all-reduce.2
  121.4 124.4 all-reduce.4
  254.1 48.2 all-gather.1
where the time goes:
time: 312 us
  waiting for transfers between devices  241 us (77%)
  other arithmetic  20.6 us (7%)
  matrix products  19.4 us (6%)
  between operations  14.5 us (5%)
  blocking collectives  10.3 us (3%)
  local copies, waits for them, and re-layouts  5.99 us (2%)
    psum x1, waiting for transfers between devices, on_device(): right_factor = lax.psum(projected, ('rep', 'shard')) / replicas  124 us
    psum x1, waiting for transfers between devices, on_device(): factor = lax.psum(local_factor, 'rep') / replicas  73.4 us
    all_gather x1, waiting for transfers between devices, on_device(): lax.all_gather(master_out.astype(jnp.bfloat16), 'rep', axis=0, tiled=True)  43.1 us
    psum x1, blocking collectives, on_device(): gram = lax.psum(gram_part, 'shard')  10.3 us
    dot_general x2, matrix products, contract_first(): lax.dot_general(left, right, (((0,), (0,)), ((), ())), precision=HIGHEST,...  7.45 us
    dot_general x1, matrix products, on_device(): jnp.dot(merged, unit_basis, precision=HIGHEST, preferred_element_type=jnp...  6.87 us
    another operation x3, other arithmetic, lower_inverse(): cholesky_lower = jnp.linalg.cholesky(gram + ridge_term * identity)  6.52 us
  transfers between devices with their start and end apart: 3, of which 3 were waited for; matrix products, arithmetic and copies ran while one was open for 2% of the time, Pallas kernels for 0%

commit v1 on v0

v1 whole, which is shorter than its diff:
```python
import functools

import jax
import jax.numpy as jnp
from jax import lax
from jax.experimental import pallas as pl
from jax.experimental.pallas import tpu as pltpu
from jax.sharding import PartitionSpec as P

HIGHEST = lax.Precision.HIGHEST
MESH = pl.DeviceIdType.MESH
beta_one = 0.9
beta_two = 0.95
learn_rate = 0.02
decay_rate = 0.1
adam_eps = 1e-08
ridge_rate = 1e-06
bf16 = jnp.bfloat16
f32 = jnp.float32


def lower_inverse(gram, order):
    rows = lax.broadcasted_iota(jnp.int32, (order, order), 0)
    cols = lax.broadcasted_iota(jnp.int32, (order, order), 1)
    eye = (rows == cols).astype(f32)
    trace = jnp.sum(gram * eye, keepdims=True)
    work = jnp.concatenate([gram + (ridge_rate / order) * trace * eye, eye], axis=1)
    below = lax.broadcasted_iota(jnp.int32, (order, 1), 0)
    for j in range(order - 1):
        pivot_row = work[j : j + 1, :]
        column = work[:, j : j + 1] * (1.0 / work[j : j + 1, j : j + 1])
        work = work - jnp.where(below > j, column, 0.0) * pivot_row
    pivots = jnp.sum(work[:, :order] * eye, axis=1, keepdims=True)
    return work[:, order:] * (1.0 / jnp.sqrt(pivots))


def split(value):
    high = value.astype(bf16)
    return high, (value - high.astype(f32)).astype(bf16)


def nn(left, right):
    return jnp.dot(left, right, preferred_element_type=f32)


def nt(left, right, precision=None):
    return lax.dot_general(
        left, right, (((1,), (1,)), ((), ())), precision=precision, preferred_element_type=f32
    )


def kernel(
    reps, shards, inner,
    g_hbm, f_hbm, w_ref, master_hbm, moment_hbm, second_hbm,
    nf_hbm, wt_hbm, master_o, moment_o, second_o, right_o,
    gv, fv, w2, acc, ft, u3, state, apx,
    fsend, frecv, fall, grams, psend, precv, qx, rall, wall,
    load_sem, state_sem, f_ss, f_rs, a_ss, a_rs, gr_ss, gr_rs, p_ss, p_rs, q_ss, q_rs, r_ss, r_rs,
    w_ss, w_rs, nf_sem, wo_sem, so_sem, ro_sem,
):
    rank = w_ref.shape[1]
    depth, cols = gv.shape
    own_rows = state.shape[1]
    cb = fsend.shape[2]
    outer = reps // inner
    me = lax.axis_index("rep")
    ms = lax.axis_index("shard")
    chunks = load_sem.shape[1]
    crows = depth // chunks

    def load(c):
        part = pl.ds(c * crows, crows)
        return (
            pltpu.make_async_copy(g_hbm.at[0, part], gv.at[part], load_sem.at[0, c]),
            pltpu.make_async_copy(f_hbm.at[0, part], fv.at[part], load_sem.at[1, c]),
        )

    for c in range(chunks):
        for copy in load(c):
            copy.start()
    state_in = [
        pltpu.make_async_copy(src, state.at[i], state_sem.at[i])
        for i, src in enumerate((master_hbm, moment_hbm, second_hbm))
    ]
    for copy in state_in:
        copy.start()

    barrier = pltpu.get_barrier_semaphore()
    for k in range(1, reps):
        pl.semaphore_signal(barrier, inc=1, device_id={"rep": lax.rem(me + k, reps)}, device_id_type=MESH)
    for k in range(1, shards):
        pl.semaphore_signal(barrier, inc=1, device_id={"shard": lax.rem(ms + k, shards)}, device_id_type=MESH)

    def remote(src, dst, send_sem, recv_sem, axis, peer):
        return pltpu.make_async_remote_copy(
            src_ref=src, dst_ref=dst, send_sem=send_sem, recv_sem=recv_sem,
            device_id={axis: peer}, device_id_type=MESH,
        )

    wh, wl = split(w_ref[...].T)
    w2[...] = jnp.concatenate([wh, wl], axis=0)
    for c in range(chunks):
        for copy in load(c):
            copy.wait()
        part = pl.ds(c * crows, crows)
        term = nn(w2[:, part], gv[part, :]) + nn(w2[:, part], fv[part, :])
        if c == 0:
            acc[...] = term
        else:
            acc[...] += term
    for r in range(reps):
        part = pl.ds(r * cb, cb)
        fsend[r] = acc[:rank, part] + acc[rank:, part]
    pl.semaphore_wait(barrier, reps + shards - 2)

    def scatter(k):
        peer = lax.rem(me + k, reps)
        return remote(fsend.at[peer], frecv.at[k], f_ss.at[k], f_rs.at[k], "rep", peer)

    for k in range(1, reps):
        scatter(k).start()
    total = fsend[me]
    for k in range(1, reps):
        scatter(k).wait_recv()
        total = total + frecv[k]
    fall[me] = total * (1.0 / reps)

    def gather(buf, ss, rs, axis, size, mine, k, sending):
        peer = lax.rem(mine + k, size) if sending else lax.rem(mine + size - k, size)
        slot = mine if sending else peer
        return remote(buf.at[slot], buf.at[slot], ss.at[k], rs.at[k], axis, lax.rem(mine + k, size))

    def start_gather(buf, ss, rs, axis, size, mine):
        for k in range(1, size):
            gather(buf, ss, rs, axis, size, mine, k, True).start()

    def wait_gather(buf, ss, rs, axis, size, mine):
        for k in range(1, size):
            gather(buf, ss, rs, axis, size, mine, k, False).wait_recv()

    start_gather(fall, a_ss, a_rs, "rep", reps, me)
    wait_gather(fall, a_ss, a_rs, "rep", reps, me)
    for r in range(reps):
        ft[:, pl.ds(r * cb, cb)] = fall[r]
    factor = ft[...]
    grams[ms] = nt(factor, factor, HIGHEST)
    start_gather(grams, gr_ss, gr_rs, "shard", shards, ms)
    wait_gather(grams, gr_ss, gr_rs, "shard", shards, ms)
    gram = grams[0]
    for s in range(1, shards):
        gram = gram + grams[s]
    inverse = lower_inverse(gram, rank)
    basis = jnp.dot(inverse, ft[...], precision=HIGHEST, preferred_element_type=f32)
    uh, ul = split(basis)
    u3[...] = jnp.concatenate([uh, ul, uh], axis=0)

    def project(peer):
        part = pl.ds(pl.multiple_of(peer * own_rows, own_rows), own_rows)
        both = nt(u3[: 2 * rank, :], gv[part, :]) + nt(u3[: 2 * rank, :], fv[part, :])
        return both[:rank] + both[rank:]

    def scatter_right(k):
        peer = lax.rem(me + k, reps)
        return remote(psend.at[peer], precv.at[k], p_ss.at[k], p_rs.at[k], "rep", peer)

    for k in range(1, reps):
        peer = lax.rem(me + k, reps)
        psend[peer] = project(peer)
        scatter_right(k).start()
    total = project(me)
    for k in range(1, reps):
        scatter_right(k).wait_recv()
        total = total + precv[k]
    qx[ms] = total
    start_gather(qx, q_ss, q_rs, "shard", shards, ms)
    wait_gather(qx, q_ss, q_rs, "shard", shards, ms)
    total = qx[0]
    for s in range(1, shards):
        total = total + qx[s]
    rall[me] = total * (1.0 / reps)
    start_gather(rall, r_ss, r_rs, "rep", reps, me)

    def approx_rows(r):
        rh, rl = split(rall[r].T)
        return nn(jnp.concatenate([rh, rh, rl], axis=1), u3[...])

    apx[...] = approx_rows(me)
    for copy in state_in:
        copy.wait()
    step_rows = 16

    def adam(i, carry):
        part = pl.ds(pl.multiple_of(i * step_rows, step_rows), step_rows)
        grad = apx[part, :]
        master = state[0, part, :]
        moment_out = beta_one * state[1, part, :] + (1.0 - beta_one) * grad
        second_out = beta_two * state[2, part, :] + (1.0 - beta_two) * grad * grad
        master_out = master - learn_rate * (
            moment_out / (jnp.sqrt(second_out) + adam_eps) + decay_rate * master
        )
        state[0, part, :] = master_out
        state[1, part, :] = moment_out
        state[2, part, :] = second_out
        wall[me, part, :] = master_out.astype(bf16)
        return carry

    lax.fori_loop(0, own_rows // step_rows, adam, 0)

    ma = lax.div(me, inner)
    mb = lax.rem(me, inner)

    def hop(block, way, peer):
        return remote(wall.at[block], wall.at[block], w_ss.at[block, way], w_rs.at[block], "rep", peer)

    def forward(a, up, down):
        block = a * inner + mb
        if up:
            @pl.when(ma + 1 < outer)
            def _():
                hop(block, 0, me + inner).start()
        if down:
            @pl.when(ma > 0)
            def _():
                hop(block, 1, me - inner).start()
        for j in range(1, inner):
            hop(block, 1 + j, ma * inner + lax.rem(mb + j, inner)).start()

    def keep(block):
        part = pl.ds(pl.multiple_of(block * own_rows, own_rows), own_rows)
        return pltpu.make_async_copy(wall.at[block], wt_hbm.at[part], wo_sem.at[block])

    forward(ma, True, True)
    keep(me).start()
    state_out = [
        pltpu.make_async_copy(state.at[i], dst, so_sem.at[i])
        for i, dst in enumerate((master_o, moment_o, second_o))
    ]
    for copy in state_out:
        copy.start()

    wait_gather(rall, r_ss, r_rs, "rep", reps, me)
    right_copy = pltpu.make_async_copy(rall, right_o, ro_sem)
    right_copy.start()

    def residue(r):
        part = pl.ds(pl.multiple_of(r * own_rows, own_rows), own_rows)
        return part, pltpu.make_async_copy(gv.at[part], nf_hbm.at[0, part], nf_sem.at[r])

    def feedback_rows(r, carry):
        part, copy = residue(r)
        merged = gv[part, :].astype(f32) + fv[part, :].astype(f32)
        gv[part, :] = (merged - approx_rows(r)).astype(bf16)
        copy.start()
        return carry

    lax.fori_loop(0, reps, feedback_rows, 0)

    for t in range(1, outer):
        @pl.when(ma - t >= 0)
        def _():
            block = (ma - t) * inner + mb
            hop(block, 0, me).wait_recv()
            forward(ma - t, True, False)
            keep(block).start()

        @pl.when(ma + t < outer)
        def _():
            block = (ma + t) * inner + mb
            hop(block, 1, me).wait_recv()
            forward(ma + t, False, True)
            keep(block).start()

    for j in range(1, inner):
        for a in range(outer):
            block = a * inner + lax.rem(mb + j, inner)
            hop(block, 1 + j, me).wait_recv()
            keep(block).start()

    for k in range(1, reps):
        scatter(k).wait_send()
        scatter_right(k).wait_send()
        gather(fall, a_ss, a_rs, "rep", reps, me, k, True).wait_send()
        gather(rall, r_ss, r_rs, "rep", reps, me, k, True).wait_send()
    for k in range(1, shards):
        gather(grams, gr_ss, gr_rs, "shard", shards, ms, k, True).wait_send()
        gather(qx, q_ss, q_rs, "shard", shards, ms, k, True).wait_send()
    for a in range(outer):
        block = a * inner + mb

        @pl.when((a <= ma) & (ma + 1 < outer))
        def _():
            hop(block, 0, me).wait_send()

        @pl.when((a >= ma) & (ma > 0))
        def _():
            hop(block, 1, me).wait_send()

        for j in range(1, inner):
            hop(block, 1 + j, me).wait_send()
    for copy in state_out:
        copy.wait()
    right_copy.wait()
    for r in range(reps):
        residue(r)[1].wait()
        keep(r).wait()


def on_device(gradient, feedback, warm_start, master, moment, second):
    reps = lax.axis_size("rep")
    shards = lax.axis_size("shard")
    inner = 2 if reps <= 8 else 8
    _, depth, cols = gradient.shape
    rank = warm_start.shape[1]
    own_rows = master.shape[0]
    cb = cols // reps
    chunks = 4
    dma = pltpu.SemaphoreType.DMA
    anywhere = pl.BlockSpec(memory_space=pl.ANY)
    new_feedback, weights, master_out, moment_out, second_out, right = pl.pallas_call(
        functools.partial(kernel, reps, shards, inner),
        out_shape=(
            jax.ShapeDtypeStruct(gradient.shape, bf16),
            jax.ShapeDtypeStruct((depth, cols), bf16),
            jax.ShapeDtypeStruct(master.shape, f32),
            jax.ShapeDtypeStruct(master.shape, f32),
            jax.ShapeDtypeStruct(master.shape, f32),
            jax.ShapeDtypeStruct((reps, rank, own_rows), f32),
        ),
        in_specs=[anywhere, anywhere, pl.BlockSpec(memory_space=pltpu.VMEM)] + [anywhere] * 3,
        out_specs=(anywhere,) * 6,
        scratch_shapes=[
            pltpu.VMEM((depth, cols), bf16),
            pltpu.VMEM((depth, cols), bf16),
            pltpu.VMEM((2 * rank, depth), bf16),
            pltpu.VMEM((2 * rank, cols), f32),
            pltpu.VMEM((rank, cols), f32),
            pltpu.VMEM((3 * rank, cols), bf16),
            pltpu.VMEM((3, own_rows, cols), f32),
            pltpu.VMEM((own_rows, cols), f32),
            pltpu.VMEM((reps, rank, cb), f32),
            pltpu.VMEM((reps, rank, cb), f32),
            pltpu.VMEM((reps, rank, cb), f32),
            pltpu.VMEM((shards, rank, rank), f32),
            pltpu.VMEM((reps, rank, own_rows), f32),
            pltpu.VMEM((reps, rank, own_rows), f32),
            pltpu.VMEM((shards, rank, own_rows), f32),
            pltpu.VMEM((reps, rank, own_rows), f32),
            pltpu.VMEM((reps, own_rows, cols), bf16),
            dma((2, chunks)),
            dma((3,)),
            dma((reps,)), dma((reps,)),
            dma((reps,)), dma((reps,)),
            dma((shards,)), dma((shards,)),
            dma((reps,)), dma((reps,)),
            dma((shards,)), dma((shards,)),
            dma((reps,)), dma((reps,)),
            dma((reps, inner + 1)), dma((reps,)),
            dma((reps,)), dma((reps,)), dma((3,)), dma(()),
        ],
        compiler_params=pltpu.CompilerParams(
            collective_id=0, has_side_effects=True, vmem_limit_bytes=40 * 1024 * 1024
        ),
    )(gradient, feedback, warm_start, master, moment, second)
    right_factor = jnp.swapaxes(right, 1, 2).reshape(depth, rank)
    return (new_feedback, weights, master_out, moment_out, second_out, right_factor)


def solution(mesh):
    return jax.shard_map(
        on_device,
        mesh=mesh,
        in_specs=(
            P("rep", None, "shard"),
            P("rep", None, "shard"),
            P(),
            P("rep", "shard"),
            P("rep", "shard"),
            P("rep", "shard"),
        ),
        out_specs=(
            P("rep", None, "shard"),
            P(None, "shard"),
            P("rep", "shard"),
            P("rep", "shard"),
            P("rep", "shard"),
            P(),
        ),
        check_vma=False,
    )
```

time: 312 us -> 88.7 us (0.28)
  waiting for transfers between devices: 241 us -> 0 us
  Pallas kernels: 0 us -> 74.5 us
  other arithmetic: 20.6 us -> 0 us
  matrix products: 19.4 us -> 0 us
  between operations: 14.5 us -> 0.66 us
  blocking collectives: 10.3 us -> 0 us
  local copies, waits for them, and re-layouts: 5.99 us -> 13.2 us
    psum x2 -> x0, waiting for transfers between devices: 198 us -> none  [the longest x1 124 us: on_device(): right_factor = lax.psum(projected, ('rep', 'shard')) / replicas]
    pallas_call x0 -> x1, Pallas kernels: none -> 74.5 us  [on_device(): pl.pallas_call(functools.partial(kernel, reps, shards, inner), out_shape=...]
    all_gather x1 -> x0, waiting for transfers between devices: 43.1 us -> none  [on_device(): lax.all_gather(master_out.astype(jnp.bfloat16), 'rep', axis=0, tiled=True)]
    dot_general x5 -> x0, matrix products: 19.2 us -> none  [the longest x2 7.45 us: contract_first(): lax.dot_general(left, right, (((0,), (0,)), ((), ())), precision=HIGHEST,...]
    another operation x5 -> x0, other arithmetic: 12.1 us -> none  [the longest x3 6.52 us: lower_inverse(): cholesky_lower = jnp.linalg.cholesky(gram + ridge_term * identity)]
    psum x1 -> x0, blocking collectives: 10.3 us -> none  [on_device(): gram = lax.psum(gram_part, 'shard')]
    unnamed x15 -> x16, local copies, waits for them, and re-layouts: 5.91 us -> 12.5 us
    broadcast_in_dim x1 -> x0, other arithmetic: 5.41 us -> none  [on_device(): new_feedback = (merged - approx).astype(jnp.bfloat16)[None]]
  transfers between devices with their start and end apart: 3 -> 0, of which waited for: 3 -> 0; matrix products, arithmetic and copies ran while one was open for 2% -> 0% of each run, Pallas kernels for 0% -> 0%
where the time goes in v1:
time: 88.7 us; the launch traced here: 88.4 us
  Pallas kernels  74.5 us (84%)
  local copies, waits for them, and re-layouts  13.2 us (15%)
    pallas_call x1, Pallas kernels, on_device(): pl.pallas_call(functools.partial(kernel, reps, shards, inner), out_shape=...  74.5 us
    unnamed x16, local copies, waits for them, and re-layouts  12.5 us

profile of v1, /device:TPU:0, one launch (start us, length us, event | category | flops | bytes accessed | tf_op | source)
XLA Modules:
  0.0 88.4 jit_solution(11900371603494555733)
XLA Ops:
  0.6 1.1 %copy.13.w_ref = f32[1024,64]{1,0:T(8,128)S(1)} copy(f32[1024,64]{0,1:T(8,128)} %param.8) | data formatting | bytes 524288 | tf_op args[2]
  1.8 0.0 copy-start
  1.8 1.6 %copy-done = bf16[1,1024,1024]{2,1,0:T(8,128)(2,1)S(1)} copy-done((bf16[1,1024,1024]{2,1,0:T(8,128)(2,1)S(1)}, bf16[1,1024,1024]{2,1,0:T(8,128)(2,1)}, u32[]{:S(2)}) %copy-start) | copy-done | bytes 2097176
  3.4 0.0 copy-start.1
  3.4 1.6 %copy-done.1 = bf16[1,1024,1024]{2,1,0:T(8,128)(2,1)S(1)} copy-done((bf16[1,1024,1024]{2,1,0:T(8,128)(2,1)S(1)}, bf16[1,1024,1024]{2,1,0:T(8,128)(2,1)}, u32[]{:S(2)}) %copy-start.1) | copy-done | bytes 2097176
  5.0 0.0 copy-start.2
  5.0 1.0 %copy-done.2 = f32[128,1024]{1,0:T(8,128)S(1)} copy-done((f32[128,1024]{1,0:T(8,128)S(1)}, f32[128,1024]{1,0:T(8,128)}, u32[]{:S(2)}) %copy-start.2) | copy-done | bytes 524312
  6.0 0.0 copy-start.3
  6.0 1.0 %copy-done.3 = f32[128,1024]{1,0:T(8,128)S(1)} copy-done((f32[128,1024]{1,0:T(8,128)S(1)}, f32[128,1024]{1,0:T(8,128)}, u32[]{:S(2)}) %copy-start.3) | copy-done | bytes 524312
  7.1 0.0 copy-start.4
  7.1 1.0 %copy-done.4 = f32[128,1024]{1,0:T(8,128)S(1)} copy-done((f32[128,1024]{1,0:T(8,128)S(1)}, f32[128,1024]{1,0:T(8,128)}, u32[]{:S(2)}) %copy-start.4) | copy-done | bytes 524312
  8.1 74.5 %shard_map.109 = (bf16[1,1024,1024]{2,1,0:T(8,128)(2,1)S(1)}, bf16[1024,1024]{1,0:T(8,128)(2,1)S(1)}, f32[128,1024]{1,0:T(8,128)S(1)}, f32[128,1024]{1,0:T(8,128...) custom-call(bf16[1,1024,1024]{2,1,0:T(8,128)(2,1)S(1)} %copy-done, bf16[1,1024,1024]{2,1,0:T(8,128)(2,1)S(1)} %copy-done.1, ...), custom_call_target="tpu_custom_call" | custom-call | tf_op jit(solution)/shard_map/pallas_call | solution.py:319
  82.7 0.7 copy_bitcast_fusion
  83.4 1.3 %copy.22 = bf16[1,1024,1024]{2,1,0:T(8,128)(2,1)} copy(bf16[1,1024,1024]{2,1,0:T(8,128)(2,1)S(1)} %get-tuple-element.24) | data formatting | bytes 4194304
  84.7 1.3 %copy.23 = bf16[1024,1024]{1,0:T(8,128)(2,1)} copy(bf16[1024,1024]{1,0:T(8,128)(2,1)S(1)} %get-tuple-element.25) | data formatting | bytes 4194304
  86.0 0.8 copy.24
  86.8 0.8 copy.25
  87.6 0.8 copy.26
Async XLA Ops:
  1.8 1.6 %copy-start = (bf16[1,1024,1024]{2,1,0:T(8,128)(2,1)S(1)}, bf16[1,1024,1024]{2,1,0:T(8,128)(2,1)}, u32[]{:S(2)}) copy-start(bf16[1,1024,1024]{2,1,0:T(8,128)(2,1)} %g_hbm.1) | copy-start | bytes 6291460
  3.4 1.6 %copy-start.1 = (bf16[1,1024,1024]{2,1,0:T(8,128)(2,1)S(1)}, bf16[1,1024,1024]{2,1,0:T(8,128)(2,1)}, u32[]{:S(2)}) copy-start(bf16[1,1024,1024]{2,1,0:T(8,128)(2,1)} %f_hbm.1) | copy-start | bytes 6291460
  5.0 1.0 %copy-start.2 = (f32[128,1024]{1,0:T(8,128)S(1)}, f32[128,1024]{1,0:T(8,128)}, u32[]{:S(2)}) copy-start(f32[128,1024]{1,0:T(8,128)} %master_hbm.1) | copy-start | bytes 1572868
  6.0 1.0 %copy-start.3 = (f32[128,1024]{1,0:T(8,128)S(1)}, f32[128,1024]{1,0:T(8,128)}, u32[]{:S(2)}) copy-start(f32[128,1024]{1,0:T(8,128)} %moment_hbm.1) | copy-start | bytes 1572868
  7.1 1.0 %copy-start.4 = (f32[128,1024]{1,0:T(8,128)S(1)}, f32[128,1024]{1,0:T(8,128)}, u32[]{:S(2)}) copy-start(f32[128,1024]{1,0:T(8,128)} %second_hbm.1) | copy-start | bytes 1572868

commit v2 on v1

v2 whole, which is shorter than its diff:
```python
import functools

import jax
import jax.numpy as jnp
from jax import lax
from jax.experimental import pallas as pl
from jax.experimental.pallas import tpu as pltpu
from jax.sharding import PartitionSpec as P

HIGHEST = lax.Precision.HIGHEST
MESH = pl.DeviceIdType.MESH
beta_one = 0.9
beta_two = 0.95
learn_rate = 0.02
decay_rate = 0.1
adam_eps = 1e-08
ridge_rate = 1e-06
bf16 = jnp.bfloat16
f32 = jnp.float32


def lower_inverse(gram, order, width=4):
    rows = lax.broadcasted_iota(jnp.int32, (order, order), 0)
    cols = lax.broadcasted_iota(jnp.int32, (order, order), 1)
    eye = (rows == cols).astype(f32)
    trace = jnp.sum(gram * eye, keepdims=True)
    work = jnp.concatenate([gram + (ridge_rate / order) * trace * eye, eye], axis=1)
    done = []
    for top in range(0, order, 8):
        height = order - top
        below = lax.broadcasted_iota(jnp.int32, (height, 2 * order), 0)
        for first in range(0, 8, width):
            pick = range(first, first + width)
            c = {k: jnp.broadcast_to(work[:, top + k : top + k + 1], work.shape) for k in pick}
            r = {k: work[k : k + 1, :] for k in pick}
            s = {(i, k): c[k][i : i + 1, :] for k in pick for i in pick if i >= k}
            terms = []
            for k in pick:
                inv = 1.0 / s[k, k]
                later = range(k + 1, first + width)
                m = {i: s[i, k] * inv for i in later}
                column = c[k] * inv
                terms.append(jnp.where(below > k, column, 0.0) * r[k])
                for i in later:
                    for l in range(k + 1, i + 1):
                        s[i, l] = s[i, l] - m[i] * s[l, k]
                    c[i] = c[i] - column * s[i, k]
                    r[i] = r[i] - m[i] * r[k]
            for term in terms:
                work = work - term
        done.append(work[:8])
        work = work[8:]
    work = jnp.concatenate(done, axis=0)
    pivots = jnp.sum(work[:, :order] * eye, axis=1, keepdims=True)
    return work[:, order:] * (1.0 / jnp.sqrt(pivots))


def split(value):
    high = value.astype(bf16)
    return high, (value - high.astype(f32)).astype(bf16)


def nn(left, right):
    return jnp.dot(left, right, preferred_element_type=f32)


def nt(left, right, precision=None):
    return lax.dot_general(
        left, right, (((1,), (1,)), ((), ())), precision=precision, preferred_element_type=f32
    )


def kernel(
    reps, shards, inner, wide,
    g_hbm, f_hbm, w_ref, master_hbm, moment_hbm, second_hbm,
    nf_hbm, wt_hbm, apx_o, right_o,
    gv, fv, w2, ft, u3, rt, state, apx,
    fsend, frecv, fall, grams, psend, precv, qx, rall, wall,
    load_sem, state_sem, f_ss, f_rs, a_ss, a_rs, gr_ss, gr_rs, p_ss, p_rs, q_ss, q_rs, r_ss, r_rs,
    w_ss, w_rs, nf_sem, wo_sem, ao_sem, ro_sem,
):
    rank = w_ref.shape[0]
    depth, cols = gv.shape
    own_rows = state.shape[1]
    cb = fsend.shape[2]
    outer = reps // inner
    me = lax.axis_index("rep")
    ms = lax.axis_index("shard")
    groups = load_sem.shape[1]
    gw = cols // groups
    per = gw // cb

    def group(k, count, size):
        return lax.rem(lax.div(me, size) + 1 + k, count)

    def load(k):
        part = pl.ds(pl.multiple_of(group(k, groups, per) * gw, gw), gw)
        return (
            pltpu.make_async_copy(g_hbm.at[0, :, part], gv.at[:, part], load_sem.at[0, k]),
            pltpu.make_async_copy(f_hbm.at[0, :, part], fv.at[:, part], load_sem.at[1, k]),
        )

    for k in range(groups):
        for copy in load(k):
            copy.start()
    state_in = [
        pltpu.make_async_copy(src, state.at[i], state_sem.at[i])
        for i, src in enumerate((master_hbm, moment_hbm, second_hbm))
    ]
    for copy in state_in:
        copy.start()

    barrier = pltpu.get_barrier_semaphore()
    for k in range(1, reps):
        pl.semaphore_signal(barrier, inc=1, device_id={"rep": lax.rem(me + k, reps)}, device_id_type=MESH)
    for k in range(1, shards):
        pl.semaphore_signal(barrier, inc=1, device_id={"shard": lax.rem(ms + k, shards)}, device_id_type=MESH)

    def remote(src, dst, send_sem, recv_sem, axis, peer):
        return pltpu.make_async_remote_copy(
            src_ref=src, dst_ref=dst, send_sem=send_sem, recv_sem=recv_sem,
            device_id={axis: peer}, device_id_type=MESH,
        )

    wh, wl = split(w_ref[...])
    w2[...] = jnp.concatenate([wh, wl], axis=0)

    def scatter(src, dst, ss, rs, peer):
        k = lax.rem(peer - me + reps, reps)
        return remote(src.at[peer], dst.at[k], ss.at[k], rs.at[k], "rep", peer)

    def scatter_group(value, base, count, width, src, dst, ss, rs):
        for q in range(count):
            peer = base + q
            src[peer] = value[:, q * width : (q + 1) * width]

            @pl.when(peer != me)
            def _():
                scatter(src, dst, ss, rs, peer).start()

    def scatter_sum(src, dst, ss, rs):
        total = src[me]
        for k in range(1, reps):
            remote(src.at[me], dst.at[k], ss.at[k], rs.at[k], "rep", lax.rem(me + k, reps)).wait_recv()
            total = total + dst[k]
        return total

    for k in range(groups):
        for copy in load(k):
            copy.wait()
        part = pl.ds(pl.multiple_of(group(k, groups, per) * gw, gw), gw)
        both = nn(w2[...], gv[:, part]) + nn(w2[...], fv[:, part])
        if k == 0:
            pl.semaphore_wait(barrier, reps + shards - 2)
        scatter_group(
            both[:rank] + both[rank:], group(k, groups, per) * per, per, cb, fsend, frecv, f_ss, f_rs
        )

    fall[me] = scatter_sum(fsend, frecv, f_ss, f_rs) * (1.0 / reps)

    def gather(buf, ss, rs, axis, size, mine, k, sending):
        peer = lax.rem(mine + k, size) if sending else lax.rem(mine + size - k, size)
        slot = mine if sending else peer
        return remote(buf.at[slot], buf.at[slot], ss.at[k], rs.at[k], axis, lax.rem(mine + k, size))

    def start_gather(buf, ss, rs, axis, size, mine):
        for k in range(1, size):
            gather(buf, ss, rs, axis, size, mine, k, True).start()

    def wait_gather(buf, ss, rs, axis, size, mine):
        for k in range(1, size):
            gather(buf, ss, rs, axis, size, mine, k, False).wait_recv()

    start_gather(fall, a_ss, a_rs, "rep", reps, me)
    wait_gather(fall, a_ss, a_rs, "rep", reps, me)
    for r in range(reps):
        ft[:, pl.ds(r * cb, cb)] = fall[r]
    factor = ft[...]
    grams[ms] = nt(factor, factor, HIGHEST)
    start_gather(grams, gr_ss, gr_rs, "shard", shards, ms)
    wait_gather(grams, gr_ss, gr_rs, "shard", shards, ms)
    gram = grams[0]
    for s in range(1, shards):
        gram = gram + grams[s]
    inverse = lower_inverse(gram, rank)
    basis = jnp.dot(inverse, ft[...], precision=HIGHEST, preferred_element_type=f32)
    uh, ul = split(basis)
    u3[...] = jnp.concatenate([uh, ul, uh], axis=0)

    many = wide // own_rows
    for k in range(depth // wide):
        index = group(k, depth // wide, many)
        part = pl.ds(pl.multiple_of(index * wide, wide), wide)
        both = nt(u3[: 2 * rank, :], gv[part, :]) + nt(u3[: 2 * rank, :], fv[part, :])
        scatter_group(
            both[:rank] + both[rank:], index * many, many, own_rows, psend, precv, p_ss, p_rs
        )
    total = scatter_sum(psend, precv, p_ss, p_rs)
    qx[ms] = total
    start_gather(qx, q_ss, q_rs, "shard", shards, ms)
    wait_gather(qx, q_ss, q_rs, "shard", shards, ms)
    total = qx[0]
    for s in range(1, shards):
        total = total + qx[s]
    rall[me] = total * (1.0 / reps)
    start_gather(rall, r_ss, r_rs, "rep", reps, me)

    def approx_rows(r):
        rh, rl = split(rall[r].T)
        return nn(jnp.concatenate([rh, rh, rl], axis=1), u3[...])

    apx[...] = approx_rows(me)
    apx_copy = pltpu.make_async_copy(apx, apx_o, ao_sem)
    apx_copy.start()
    ma = lax.div(me, inner)
    mb = lax.rem(me, inner)
    half_rows = own_rows // 2
    has_up = ma + 1 < outer
    has_down = ma > 0

    def hop(block, half, way, peer):
        part = wall.at[block, pl.ds(half * half_rows, half_rows)]
        return remote(part, part, w_ss.at[block, half, way], w_rs.at[block, half], "rep", peer)

    def across(block, half):
        for j in range(1, inner):
            hop(block, half, 1 + j, ma * inner + lax.rem(mb + j, inner)).start()

    def along(block, half, up, down):
        if up:
            @pl.when(has_up)
            def _():
                hop(block, half, 0, me + inner).start()
        if down:
            @pl.when(has_down)
            def _():
                hop(block, half, 1, me - inner).start()

    def keep(block, half):
        part = pl.ds(pl.multiple_of(block * own_rows + half * half_rows, half_rows), half_rows)
        src = wall.at[block, pl.ds(half * half_rows, half_rows)]
        return pltpu.make_async_copy(src, wt_hbm.at[part], wo_sem.at[block, half])

    step_rows = 16
    for half in range(2):

        def adam(i, carry):
            part = pl.ds(pl.multiple_of(half * half_rows + i * step_rows, step_rows), step_rows)
            grad = apx[part, :]
            master = state[0, part, :]
            moment_out = beta_one * state[1, part, :] + (1.0 - beta_one) * grad
            second_out = beta_two * state[2, part, :] + (1.0 - beta_two) * grad * grad
            master_out = master - learn_rate * (
                moment_out / (jnp.sqrt(second_out) + adam_eps) + decay_rate * master
            )
            wall[me, part, :] = master_out.astype(bf16)
            return carry

        if half == 0:
            for copy in state_in:
                copy.wait()
        lax.fori_loop(0, half_rows // step_rows, adam, 0)
        along(me, half, True, True)
        across(me, half)
        keep(me, half).start()

    def pass_on(t, half):
        for a, up in ((ma - t, True), (ma + t, False)):
            @pl.when((a >= 0) & (a < outer))
            def _():
                block = a * inner + mb
                hop(block, half, 0, me).wait_recv()
                along(block, half, up, not up)
                if not (t == 1 and half == 1):
                    across(block, half)
                keep(block, half).start()

    if outer > 1:
        pass_on(1, 0)
        pass_on(1, 1)
    for j in range(1, inner):
        block = ma * inner + lax.rem(mb + j, inner)
        hop(block, 1, 0, me).wait_recv()
        along(block, 1, True, True)
        keep(block, 1).start()

    wait_gather(rall, r_ss, r_rs, "rep", reps, me)
    for r in range(reps):
        rt[:, pl.ds(r * own_rows, own_rows)] = rall[r]
    right_copy = pltpu.make_async_copy(rt, right_o, ro_sem)
    right_copy.start()

    def residue(r):
        part = pl.ds(pl.multiple_of(r * own_rows, own_rows), own_rows)
        return part, pltpu.make_async_copy(gv.at[part], nf_hbm.at[0, part], nf_sem.at[r])

    def feedback_rows(r, carry):
        part, copy = residue(r)
        merged = gv[part, :].astype(f32) + fv[part, :].astype(f32)
        gv[part, :] = (merged - approx_rows(r)).astype(bf16)
        copy.start()
        return carry

    lax.fori_loop(0, reps, feedback_rows, 0)

    for t in range(2, outer):
        for half in range(2):
            pass_on(t, half)

    for a in range(outer):
        for j in range(1, inner):
            block = a * inner + lax.rem(mb + j, inner)
            hop(block, 0, 0, me).wait_recv()
            keep(block, 0).start()

            @pl.when(a != ma)
            def _():
                hop(block, 1, 0, me).wait_recv()
                keep(block, 1).start()

    for k in range(1, reps):
        peer = lax.rem(me + k, reps)
        scatter(fsend, frecv, f_ss, f_rs, peer).wait_send()
        scatter(psend, precv, p_ss, p_rs, peer).wait_send()
        gather(fall, a_ss, a_rs, "rep", reps, me, k, True).wait_send()
        gather(rall, r_ss, r_rs, "rep", reps, me, k, True).wait_send()
    for k in range(1, shards):
        gather(grams, gr_ss, gr_rs, "shard", shards, ms, k, True).wait_send()
        gather(qx, q_ss, q_rs, "shard", shards, ms, k, True).wait_send()

    def sent(block, half, way):
        hop(block, half, way, me).wait_send()

    for a in range(outer):
        block = a * inner + mb
        for half in range(2):
            @pl.when((a <= ma) & has_up)
            def _():
                sent(block, half, 0)

            @pl.when((a >= ma) & has_down)
            def _():
                sent(block, half, 1)

            for j in range(1, inner):
                if half == 0:
                    sent(block, half, 1 + j)
                else:
                    @pl.when((a != ma - 1) & (a != ma + 1))
                    def _():
                        sent(block, half, 1 + j)

    for j in range(1, inner):
        block = ma * inner + lax.rem(mb + j, inner)

        @pl.when(has_up)
        def _():
            sent(block, 1, 0)

        @pl.when(has_down)
        def _():
            sent(block, 1, 1)

    apx_copy.wait()
    right_copy.wait()
    for r in range(reps):
        residue(r)[1].wait()
        keep(r, 0).wait()
        keep(r, 1).wait()


def on_device(gradient, feedback, warm_start, master, moment, second):
    reps = lax.axis_size("rep")
    shards = lax.axis_size("shard")
    inner = 2 if reps <= 8 else 8
    _, depth, cols = gradient.shape
    rank = warm_start.shape[1]
    own_rows = master.shape[0]
    cb = cols // reps
    wide = max(256, own_rows)
    groups = cols // max(256, cb)
    dma = pltpu.SemaphoreType.DMA
    anywhere = pl.BlockSpec(memory_space=pl.ANY)
    hbm = pl.BlockSpec(memory_space=pltpu.HBM)
    new_feedback, weights, grad_rows, right = pl.pallas_call(
        functools.partial(kernel, reps, shards, inner, wide),
        out_shape=(
            jax.ShapeDtypeStruct(gradient.shape, bf16),
            jax.ShapeDtypeStruct((depth, cols), bf16),
            jax.ShapeDtypeStruct(master.shape, f32),
            jax.ShapeDtypeStruct((rank, depth), f32),
        ),
        in_specs=[hbm, hbm, pl.BlockSpec(memory_space=pltpu.VMEM)] + [hbm] * 3,
        out_specs=(anywhere,) * 4,
        scratch_shapes=[
            pltpu.VMEM((depth, cols), bf16),
            pltpu.VMEM((depth, cols), bf16),
            pltpu.VMEM((2 * rank, depth), bf16),
            pltpu.VMEM((rank, cols), f32),
            pltpu.VMEM((3 * rank, cols), bf16),
            pltpu.VMEM((rank, depth), f32),
            pltpu.VMEM((3, own_rows, cols), f32),
            pltpu.VMEM((own_rows, cols), f32),
            pltpu.VMEM((reps, rank, cb), f32),
            pltpu.VMEM((reps, rank, cb), f32),
            pltpu.VMEM((reps, rank, cb), f32),
            pltpu.VMEM((shards, rank, rank), f32),
            pltpu.VMEM((reps, rank, own_rows), f32),
            pltpu.VMEM((reps, rank, own_rows), f32),
            pltpu.VMEM((shards, rank, own_rows), f32),
            pltpu.VMEM((reps, rank, own_rows), f32),
            pltpu.VMEM((reps, own_rows, cols), bf16),
            dma((2, groups)),
            dma((3,)),
            dma((reps,)), dma((reps,)),
            dma((reps,)), dma((reps,)),
            dma((shards,)), dma((shards,)),
            dma((reps,)), dma((reps,)),
            dma((shards,)), dma((shards,)),
            dma((reps,)), dma((reps,)),
            dma((reps, 2, inner + 1)), dma((reps, 2)),
            dma((reps,)), dma((reps, 2)), dma(()), dma(()),
        ],
        compiler_params=pltpu.CompilerParams(
            collective_id=0, has_side_effects=True, vmem_limit_bytes=60 * 1024 * 1024
        ),
    )(gradient, feedback, warm_start.T, master, moment, second)
    moment_out = beta_one * moment + (1.0 - beta_one) * grad_rows
    second_out = beta_two * second + (1.0 - beta_two) * grad_rows * grad_rows
    master_out = master - learn_rate * (
        moment_out / (jnp.sqrt(second_out) + adam_eps) + decay_rate * master
    )
    return (new_feedback, weights, master_out, moment_out, second_out, right.T)


def solution(mesh):
    return jax.shard_map(
        on_device,
        mesh=mesh,
        in_specs=(
            P("rep", None, "shard"),
            P("rep", None, "shard"),
            P(),
            P("rep", "shard"),
            P("rep", "shard"),
            P("rep", "shard"),
        ),
        out_specs=(
            P("rep", None, "shard"),
            P(None, "shard"),
            P("rep", "shard"),
            P("rep", "shard"),
            P("rep", "shard"),
            P(),
        ),
        check_vma=False,
    )
```

time: 88.7 us -> 79 us (0.89)
  local copies, waits for them, and re-layouts: 13.2 us -> 4.39 us
  Pallas kernels: 74.5 us -> 71.1 us
  other arithmetic: 0 us -> 2.57 us
    unnamed x16 -> x15, local copies, waits for them, and re-layouts: 12.5 us -> 4.39 us
    pallas_call x1, Pallas kernels: 74.5 us -> 71.1 us  [on_device(): pl.pallas_call(functools.partial(kernel, reps, shards, inner, wide), out_...]
    sub x0 -> x1, other arithmetic: none -> 2.57 us  [on_device(): master - learn_rate * (moment_out / (jnp.sqrt(second_out) + adam_eps) + d...]
where the time goes in v2:
time: 79 us; the launch traced here: 78.8 us
  Pallas kernels  71.1 us (90%)
  local copies, waits for them, and re-layouts  4.39 us (6%)
  other arithmetic  2.57 us (3%)
    pallas_call x1, Pallas kernels, on_device(): pl.pallas_call(functools.partial(kernel, reps, shards, inner, wide), out_...  71.1 us
    unnamed x15, local copies, waits for them, and re-layouts  4.39 us
    sub x1, other arithmetic, on_device(): master - learn_rate * (moment_out / (jnp.sqrt(second_out) + adam_eps) + d...  2.57 us

profile of v2, /device:TPU:0, one launch (start us, length us, event | category | flops | bytes accessed | tf_op | source)
XLA Modules:
  0.0 78.8 jit_solution(13787779125590592505)
XLA Ops:
  0.6 0.0 copy-start
  0.6 0.0 copy-start.1
  0.7 0.0 copy-start.2
  0.7 71.1 %shard_map.109 = (bf16[1,1024,1024]{2,1,0:T(8,128)(2,1)}, bf16[1024,1024]{1,0:T(8,128)(2,1)}, f32[128,1024]{1,0:T(8,128)}, f32[64,1024]{1,0:T(8,128)}) custom-call(bf16[1,1024,1024]{2,1,0:T(8,128)(2,1)} %g_hbm.1, bf16[1,1024,1024]{2,1,0:T(8,128)(2,1)} %f_hbm.1, f32[64,1024]{1,0:T(8,128)} %bitcast.2, f32[128,1024]{1,0:T(8,128)} %master_hbm.1, ...), custom_call_target="tpu_custom_call" | custom-call | tf_op jit(solution)/shard_map/pallas_call | solution.py:385
  71.8 0.0 copy-start.4
  71.8 0.0 copy-done
  71.8 0.0 copy-done.1
  71.8 0.0 copy-done.2
  71.8 2.6 %multiply_subtract_fusion = (f32[128,1024]{1,0:T(8,128)}, f32[128,1024]{1,0:T(8,128)}, f32[128,1024]{1,0:T(8,128)}) fusion(f32[128,1024]{1,0:T(8,128)S(1)} %copy-done, f32[128,1024]{1,0:T(8,128)} %get-tuple-element.12, f32[128,1024]{1,0:T(8,128)S(1)} %copy-done.2, f32[128,1024]{1,0:T(8,128)S(1)} %copy-done.1), kind=kLoop, calls=%fused_computation.2 | loop fusion | flops 1703936 | bytes 3670016 | tf_op jit(solution)/shard_map/sub | solution.py:430
  74.4 0.0 copy-done.4
  74.4 0.0 copy-start.3
  74.4 1.3 %copy.15 = bf16[1,1024,1024]{2,1,0:T(8,128)(2,1)} copy(bf16[1,1024,1024]{2,1,0:T(8,128)(2,1)S(1)} %copy-done.4) | data formatting | bytes 4194304
  75.7 1.0 %copy-done.3 = bf16[1024,1024]{1,0:T(8,128)(2,1)S(1)} copy-done((bf16[1024,1024]{1,0:T(8,128)(2,1)S(1)}, bf16[1024,1024]{1,0:T(8,128)(2,1)}, u32[]{:S(2)}) %copy-start.3) | copy-done | bytes 2097176
  76.7 0.0 copy-start.5
  76.7 1.3 %copy.16 = bf16[1024,1024]{1,0:T(8,128)(2,1)} copy(bf16[1024,1024]{1,0:T(8,128)(2,1)S(1)} %copy-done.3) | data formatting | bytes 4194304
  78.1 0.0 copy-done.5
  78.1 0.7 copy.17
Async XLA Ops:
  0.6 71.2 %copy-start = (f32[128,1024]{1,0:T(8,128)S(1)}, f32[128,1024]{1,0:T(8,128)}, u32[]{:S(2)}) copy-start(f32[128,1024]{1,0:T(8,128)} %master_hbm.1) | copy-start | bytes 1572868
  0.6 71.2 %copy-start.1 = (f32[128,1024]{1,0:T(8,128)S(1)}, f32[128,1024]{1,0:T(8,128)}, u32[]{:S(2)}) copy-start(f32[128,1024]{1,0:T(8,128)} %moment_hbm.1) | copy-start | bytes 1572868
  0.7 71.2 %copy-start.2 = (f32[128,1024]{1,0:T(8,128)S(1)}, f32[128,1024]{1,0:T(8,128)}, u32[]{:S(2)}) copy-start(f32[128,1024]{1,0:T(8,128)} %second_hbm.1) | copy-start | bytes 1572868
  71.8 2.6 %copy-start.4 = (bf16[1,1024,1024]{2,1,0:T(8,128)(2,1)S(1)}, bf16[1,1024,1024]{2,1,0:T(8,128)(2,1)}, u32[]{:S(2)}) copy-start(bf16[1,1024,1024]{2,1,0:T(8,128)(2,1)} %get-tuple-element.23) | copy-start | bytes 6291460
  74.4 2.3 %copy-start.3 = (bf16[1024,1024]{1,0:T(8,128)(2,1)S(1)}, bf16[1024,1024]{1,0:T(8,128)(2,1)}, u32[]{:S(2)}) copy-start(bf16[1024,1024]{1,0:T(8,128)(2,1)} %get-tuple-element.24) | copy-start | bytes 6291460
  76.7 1.3 %copy-start.5 = (f32[64,1024]{1,0:T(8,128)S(1)}, f32[64,1024]{1,0:T(8,128)}, u32[]{:S(2)}) copy-start(f32[64,1024]{1,0:T(8,128)} %get-tuple-element.13) | copy-start | bytes 786436

commit v3 on v2

--- a/solution.py
+++ b/solution.py
@@ -75,8 +75,8 @@
     g_hbm, f_hbm, w_ref, master_hbm, moment_hbm, second_hbm,
     nf_hbm, wt_hbm, apx_o, right_o,
     gv, fv, w2, ft, u3, rt, state, apx,
-    fsend, frecv, fall, grams, psend, precv, qx, rall, wall,
-    load_sem, state_sem, f_ss, f_rs, a_ss, a_rs, gr_ss, gr_rs, p_ss, p_rs, q_ss, q_rs, r_ss, r_rs,
+    fsend, frecv, fall, grams, gramr, psend, precv, qx, rall, wall,
+    load_sem, state_sem, f_ss, f_rs, a_ss, a_rs, gr_ss, gr_rs, gg_ss, gg_rs, p_ss, p_rs, q_ss, q_rs, r_ss, r_rs,
     w_ss, w_rs, nf_sem, wo_sem, ao_sem, ro_sem,
 ):
     rank = w_ref.shape[0]
@@ -156,7 +156,8 @@
             both[:rank] + both[rank:], group(k, groups, per) * per, per, cb, fsend, frecv, f_ss, f_rs
         )
 
-    fall[me] = scatter_sum(fsend, frecv, f_ss, f_rs) * (1.0 / reps)
+    block = scatter_sum(fsend, frecv, f_ss, f_rs) * (1.0 / reps)
+    fall[me] = block
 
     def gather(buf, ss, rs, axis, size, mine, k, sending):
         peer = lax.rem(mine + k, size) if sending else lax.rem(mine + size - k, size)
@@ -171,18 +172,26 @@
         for k in range(1, size):
             gather(buf, ss, rs, axis, size, mine, k, False).wait_recv()
 
+    half_rank = rank // 2
+    terms = nt(block, block, HIGHEST)
+    grams[ms] = jnp.concatenate([terms[:half_rank], terms[half_rank:]], axis=1)
+    start_gather(grams, gr_ss, gr_rs, "shard", shards, ms)
+    wait_gather(grams, gr_ss, gr_rs, "shard", shards, ms)
+    packed = grams[0]
+    for s in range(1, shards):
+        packed = packed + grams[s]
+    gramr[me] = packed
+    start_gather(gramr, gg_ss, gg_rs, "rep", reps, me)
     start_gather(fall, a_ss, a_rs, "rep", reps, me)
+    wait_gather(gramr, gg_ss, gg_rs, "rep", reps, me)
+    packed = gramr[0]
+    for r in range(1, reps):
+        packed = packed + gramr[r]
+    gram = jnp.concatenate([packed[:, :rank], packed[:, rank:]], axis=0)
+    inverse = lower_inverse(gram, rank)
     wait_gather(fall, a_ss, a_rs, "rep", reps, me)
     for r in range(reps):
         ft[:, pl.ds(r * cb, cb)] = fall[r]
-    factor = ft[...]
-    grams[ms] = nt(factor, factor, HIGHEST)
-    start_gather(grams, gr_ss, gr_rs, "shard", shards, ms)
-    wait_gather(grams, gr_ss, gr_rs, "shard", shards, ms)
-    gram = grams[0]
-    for s in range(1, shards):
-        gram = gram + grams[s]
-    inverse = lower_inverse(gram, rank)
     basis = jnp.dot(inverse, ft[...], precision=HIGHEST, preferred_element_type=f32)
     uh, ul = split(basis)
     u3[...] = jnp.concatenate([uh, ul, uh], axis=0)
@@ -275,35 +284,45 @@
                     across(block, half)
                 keep(block, half).start()
 
+    def residue(r):
+        part = pl.ds(pl.multiple_of(r * own_rows, own_rows), own_rows)
+        return part, pltpu.make_async_copy(gv.at[part], nf_hbm.at[0, part], nf_sem.at[r])
+
+    def feedback_rows(r, carry):
+        part, copy = residue(r)
+        merged = gv[part, :].astype(f32) + fv[part, :].astype(f32)
+        gv[part, :] = (merged - approx_rows(r)).astype(bf16)
+        copy.start()
+        return carry
+
+    stages = 4
+
+    def feedback(stage):
+        lax.fori_loop(reps * stage // stages, reps * (stage + 1) // stages, feedback_rows, 0)
+
     if outer > 1:
         pass_on(1, 0)
+    wait_gather(rall, r_ss, r_rs, "rep", reps, me)
+    for r in range(reps):
+        rt[:, pl.ds(r * own_rows, own_rows)] = rall[r]
+    right_copy = pltpu.make_async_copy(rt, right_o, ro_sem)
+    right_copy.start()
+    feedback(0)
+    if outer > 1:
         pass_on(1, 1)
     for j in range(1, inner):
         block = ma * inner + lax.rem(mb + j, inner)
         hop(block, 1, 0, me).wait_recv()
         along(block, 1, True, True)
         keep(block, 1).start()
-
-    wait_gather(rall, r_ss, r_rs, "rep", reps, me)
-    for r in range(reps):
-        rt[:, pl.ds(r * own_rows, own_rows)] = rall[r]
-    right_copy = pltpu.make_async_copy(rt, right_o, ro_sem)
-    right_copy.start()
-
-    def residue(r):
-        part = pl.ds(pl.multiple_of(r * own_rows, own_rows), own_rows)
-        return part, pltpu.make_async_copy(gv.at[part], nf_hbm.at[0, part], nf_sem.at[r])
-
-    def feedback_rows(r, carry):
-        part, copy = residue(r)
-        merged = gv[part, :].astype(f32) + fv[part, :].astype(f32)
-        gv[part, :] = (merged - approx_rows(r)).astype(bf16)
-        copy.start()
-        return carry
-
-    lax.fori_loop(0, reps, feedback_rows, 0)
-
-    for t in range(2, outer):
+    feedback(1)
+    if outer > 2:
+        pass_on(2, 0)
+    feedback(2)
+    if outer > 2:
+        pass_on(2, 1)
+    feedback(3)
+    for t in range(3, outer):
         for half in range(2):
             pass_on(t, half)
 
@@ -324,6 +343,7 @@
         scatter(psend, precv, p_ss, p_rs, peer).wait_send()
         gather(fall, a_ss, a_rs, "rep", reps, me, k, True).wait_send()
         gather(rall, r_ss, r_rs, "rep", reps, me, k, True).wait_send()
+        gather(gramr, gg_ss, gg_rs, "rep", reps, me, k, True).wait_send()
     for k in range(1, shards):
         gather(grams, gr_ss, gr_rs, "shard", shards, ms, k, True).wait_send()
         gather(qx, q_ss, q_rs, "shard", shards, ms, k, True).wait_send()
@@ -367,6 +387,63 @@
         residue(r)[1].wait()
         keep(r, 0).wait()
         keep(r, 1).wait()
+
+
+def finish(
+    nf_i, wt_i, right_i, apx, master, moment, second,
+    nf_o, wt_o, right_o, master_o, moment_o, second_o,
+    grad_v, state, big_sem, right_sem, in_sem, out_sem,
+):
+    pieces = in_sem.shape[1]
+    rows = grad_v.shape[0] // pieces
+    depth = wt_i.shape[0]
+    big = depth // big_sem.shape[1]
+
+    def load(p):
+        part = pl.ds(p * rows, rows)
+        into = (grad_v.at[part], state.at[0, part], state.at[1, part], state.at[2, part])
+        return [
+            pltpu.make_async_copy(src.at[part], dst, in_sem.at[i, p])
+            for i, (src, dst) in enumerate(zip((apx, master, moment, second), into))
+        ]
+
+    def store(p):
+        part = pl.ds(p * rows, rows)
+        return [
+            pltpu.make_async_copy(state.at[i, part], dst.at[part], out_sem.at[i, p])
+            for i, dst in enumerate((master_o, moment_o, second_o))
+        ]
+
+    moves = [pltpu.make_async_copy(right_i, right_o, right_sem)]
+    for p in range(big_sem.shape[1]):
+        part = pl.ds(p * big, big)
+        moves.append(pltpu.make_async_copy(nf_i.at[0, part], nf_o.at[0, part], big_sem.at[0, p]))
+        moves.append(pltpu.make_async_copy(wt_i.at[part], wt_o.at[part], big_sem.at[1, p]))
+    for p in range(pieces):
+        for copy in load(p):
+            copy.start()
+    for copy in moves:
+        copy.start()
+    for p in range(pieces):
+        for copy in load(p):
+            copy.wait()
+        part = pl.ds(p * rows, rows)
+        grad = grad_v[part, :]
+        master_in = state[0, part, :]
+        moment_out = beta_one * state[1, part, :] + (1.0 - beta_one) * grad
+        second_out = beta_two * state[2, part, :] + (1.0 - beta_two) * grad * grad
+        state[0, part, :] = master_in - learn_rate * (
+            moment_out / (jnp.sqrt(second_out) + adam_eps) + decay_rate * master_in
+        )
+        state[1, part, :] = moment_out
+        state[2, part, :] = second_out
+        for copy in store(p):
+            copy.start()
+    for p in range(pieces):
+        for copy in store(p):
+            copy.wait()
+    for copy in moves:
+        copy.wait()
 
 
 def on_device(gradient, feedback, warm_start, master, moment, second):
@@ -404,7 +481,8 @@
             pltpu.VMEM((reps, rank, cb), f32),
             pltpu.VMEM((reps, rank, cb), f32),
             pltpu.VMEM((reps, rank, cb), f32),
-            pltpu.VMEM((shards, rank, rank), f32),
+            pltpu.VMEM((shards, rank // 2, 2 * rank), f32),
+            pltpu.VMEM((reps, rank // 2, 2 * rank), f32),
             pltpu.VMEM((reps, rank, own_rows), f32),
             pltpu.VMEM((reps, rank, own_rows), f32),
             pltpu.VMEM((shards, rank, own_rows), f32),
@@ -416,6 +494,7 @@
             dma((reps,)), dma((reps,)),
             dma((shards,)), dma((shards,)),
             dma((reps,)), dma((reps,)),
+            dma((reps,)), dma((reps,)),
             dma((shards,)), dma((shards,)),
             dma((reps,)), dma((reps,)),
             dma((reps, 2, inner + 1)), dma((reps, 2)),
@@ -425,11 +504,26 @@
             collective_id=0, has_side_effects=True, vmem_limit_bytes=60 * 1024 * 1024
         ),
     )(gradient, feedback, warm_start.T, master, moment, second)
-    moment_out = beta_one * moment + (1.0 - beta_one) * grad_rows
-    second_out = beta_two * second + (1.0 - beta_two) * grad_rows * grad_rows
-    master_out = master - learn_rate * (
-        moment_out / (jnp.sqrt(second_out) + adam_eps) + decay_rate * master
-    )
+    pieces, moves = 4, 8
+    new_feedback, weights, right, master_out, moment_out, second_out = pl.pallas_call(
+        finish,
+        out_shape=(
+            jax.ShapeDtypeStruct(gradient.shape, bf16),
+            jax.ShapeDtypeStruct((depth, cols), bf16),
+            jax.ShapeDtypeStruct((rank, depth), f32),
+            jax.ShapeDtypeStruct(master.shape, f32),
+            jax.ShapeDtypeStruct(master.shape, f32),
+            jax.ShapeDtypeStruct(master.shape, f32),
+        ),
+        in_specs=[hbm] * 7,
+        out_specs=(hbm,) * 6,
+        scratch_shapes=[
+            pltpu.VMEM((own_rows, cols), f32),
+            pltpu.VMEM((3, own_rows, cols), f32),
+            dma((2, moves)), dma(()), dma((4, pieces)), dma((3, pieces)),
+        ],
+        compiler_params=pltpu.CompilerParams(vmem_limit_bytes=60 * 1024 * 1024),
+    )(new_feedback, weights, right, grad_rows, master, moment, second)
     return (new_feedback, weights, master_out, moment_out, second_out, right.T)
 
 

time: 79 us -> 209 us (2.65)
  Pallas kernels: 71.1 us -> 208 us
  local copies, waits for them, and re-layouts: 4.39 us -> 0 us
  other arithmetic: 2.57 us -> 0 us
    pallas_call x0 -> x1, Pallas kernels: none -> 137 us  [on_device(): pl.pallas_call(finish, out_shape=(jax.ShapeDtypeStruct(gradient.shape, bf...]
    unnamed x15 -> x0, local copies, waits for them, and re-layouts: 4.39 us -> none
    sub x1 -> x0, other arithmetic: 2.57 us -> none  [on_device(): master - learn_rate * (moment_out / (jnp.sqrt(second_out) + adam_eps) + d...]
where the time goes in v3:
time: 209 us
  Pallas kernels  208 us (100%)
    pallas_call x1, Pallas kernels, on_device(): pl.pallas_call(finish, out_shape=(jax.ShapeDtypeStruct(gradient.shape, bf...  137 us
    pallas_call x1, Pallas kernels, on_device(): pl.pallas_call(functools.partial(kernel, reps, shards, inner, wide), out_...  71.7 us

profile of v3, /device:TPU:0, one launch (start us, length us, event | category | flops | bytes accessed | tf_op | source)
XLA Modules:
  0.0 208.9 jit_solution(7162947925591177257)
XLA Ops:
  0.6 71.7 %shard_map.109 = (bf16[1,1024,1024]{2,1,0:T(8,128)(2,1)}, bf16[1024,1024]{1,0:T(8,128)(2,1)}, f32[128,1024]{1,0:T(8,128)}, f32[64,1024]{1,0:T(8,128)}) custom-call(bf16[1,1024,1024]{2,1,0:T(8,128)(2,1)} %g_hbm.1, bf16[1,1024,1024]{2,1,0:T(8,128)(2,1)} %f_hbm.1, f32[64,1024]{1,0:T(8,128)} %bitcast.2, f32[128,1024]{1,0:T(8,128)} %master.1, ...), custom_call_target="tpu_custom_call" | custom-call | tf_op jit(solution)/shard_map/pallas_call | solution.py:462
  72.3 136.5 %shard_map.110 = (bf16[1,1024,1024]{2,1,0:T(8,128)(2,1)}, bf16[1024,1024]{1,0:T(8,128)(2,1)}, f32[64,1024]{1,0:T(8,128)}, f32[128,1024]{1,0:T(8,128)}, f32[128,1024]{1,0:T(8,128)}, /*index=5*/f32[128,1024]{1,0:T(8,128)}) custom-call(bf16[1,1024,1024]{2,1,0:T(8,128)(2,1)} %get-tuple-element.16.nf_i, bf16[1024,1024]{1,0:T(8,128)(2,1)} %get-tuple-element.17.wt_i, ...), custom_call_target="tpu_custom_call" | custom-call | tf_op jit(solution)/shard_map/pallas_call | solution.py:508
